TPU v7x, 32 devices: a whole 2x2x4 slice. The times are simulated.
32 devices in a mesh: row: 4 (over y, core), col: 8 (over z, x).
Axes of the slice: x: 2, y: 2, z: 4, core: 2. Of those that a mesh axis runs over, the one named last changes fastest.
Arguments:
- left_values: bfloat16 [4096, 1024], P('col', 'row'), may hold values from 0.1 to 18, as said below
- left_pattern: int32 [32, 8], replicated, may hold values from 0 to 1, as said below
- right_values: bfloat16 [1024, 4096], P('col', 'row'), may hold values from 0.099609375 to 1
- right_pattern: int32 [8, 32], replicated, may hold values from 0 to 1, as said below
Outputs:
- flow: float32 [4096, 4096], P('col', 'row')
Inputs may be any that keep to these rules, and one draw needn't show every extreme that they name: left_pattern[i, i % 8] is 1 for every block row i; in every block row, each aligned group of 2 block columns holds at most 1 ones, and some group holds exactly 1. right_pattern[j % 8, j] is 1 for every block column j; in every block row, each aligned group of 8 block columns holds at most 4 ones, and some group holds exactly 4. `left_values`: positive entries.
All inputs are finite; a program needn't handle non-finite values.
Results may differ from a plain program's by a relative error of at most 0.0003.
Values may be sent and summed in bfloat16 or wider, within the bound.
A program may use at most 64 MiB of HBM per device.

v0:
```python
import jax
import jax.numpy as jnp
from jax import lax
from jax.sharding import PartitionSpec as P

BLOCK = 128


def expand(values, pattern):
    block_rows, block_cols = pattern.shape
    height, width = values.shape
    shaped = values.reshape(block_rows, height // block_rows, block_cols, width // block_cols)
    masked = shaped * pattern.astype(values.dtype)[:, None, :, None]
    return masked.reshape(height, width)


def shards(left_values, left_pattern, right_values, right_pattern):
    col_index = lax.axis_index("col")
    row_index = lax.axis_index("row")
    row_count = lax.axis_size("row")
    rows_local, inner_local = left_values.shape
    left_blocks = rows_local // BLOCK
    inner_left_blocks = inner_local // BLOCK
    left_mask = lax.dynamic_slice(
        left_pattern,
        (col_index * left_blocks, row_index * inner_left_blocks),
        (left_blocks, inner_left_blocks),
    )
    masked_left = expand(left_values, left_mask)
    left_slots = max(1, inner_left_blocks // 2)
    my_rows = lax.dynamic_slice_in_dim(left_pattern, col_index * left_blocks, left_blocks, 0)
    grouped_rows = my_rows.reshape(left_blocks, row_count, inner_left_blocks)
    left_order = jnp.argsort(1 - grouped_rows, axis=2, stable=True)[:, :, :left_slots]
    left_selector = (
        left_order[:, :, :, None] == jnp.arange(inner_left_blocks)[None, None, None, :]
    ).astype(jnp.bfloat16)
    own_left = lax.dynamic_index_in_dim(left_selector, row_index, 1, keepdims=False)
    shaped_left = masked_left.reshape(left_blocks, BLOCK, inner_left_blocks, BLOCK)
    packed_left = jnp.einsum(
        "idkn,isk->idsn", shaped_left, own_left, preferred_element_type=jnp.bfloat16
    )
    gathered_left = lax.all_gather(packed_left, "row", axis=2, tiled=True)
    gathered_left = gathered_left.reshape(left_blocks, BLOCK, row_count, left_slots, BLOCK)
    unpacked_left = jnp.einsum(
        "idrsn,irsk->idrkn", gathered_left, left_selector, preferred_element_type=jnp.bfloat16
    )
    whole_left = unpacked_left.reshape(rows_local, row_count * inner_local)
    inner_rows, cols_local = right_values.shape
    right_blocks = inner_rows // BLOCK
    col_blocks = cols_local // BLOCK
    right_mask = lax.dynamic_slice(
        right_pattern,
        (col_index * right_blocks, row_index * col_blocks),
        (right_blocks, col_blocks),
    )
    masked_right = expand(right_values, right_mask)
    product = jnp.dot(
        whole_left,
        lax.all_gather(masked_right, "col", axis=0, tiled=True),
        preferred_element_type=jnp.float32,
    )
    inflated = product * product
    totals = lax.psum(jnp.sum(inflated, axis=0), "col")
    column_mean = totals / (rows_local * lax.axis_size("col"))
    return inflated / column_mean[None, :]


def solution(mesh):
    return jax.shard_map(
        shards,
        mesh=mesh,
        in_specs=(P("col", "row"), P(), P("col", "row"), P()),
        out_specs=P("col", "row"),
        check_vma=False,
    )
```

profile of v0, /device:TPU:0, one launch (start us, length us, event | category | flops | bytes accessed | tf_op | source)
XLA Modules:
  0.0 91.8 jit_solution(6751965019556534763)
XLA Ops:
  6.5 0.0 all-gather.3.cloned.1.call-start
  6.5 0.8 convert_bitcast_fusion
  7.3 0.1 broadcast_bitcast_fusion
  7.4 1.7 %broadcast_multiply_fusion = bf16[128,1024]{1,0:T(8,128)(2,1)} fusion(bf16[128,1024]{1,0:T(8,128)(2,1)} %param.6, bf16[1024]{0:T(1024)(128)(2,1)S(1)} %broadcast_bitcast_fusion), kind=kLoop, calls=%fused_computation.5 | loop fusion | flops 131072 | bytes 526336 | tf_op jit(solution)/shard_map/mul | solution.py:13
  9.0 0.0 all-gather.3.cloned.1.call-update
  9.1 0.8 dynamic-slice_convert_fusion
  9.8 0.1 copy.9
  10.0 0.8 dynamic-slice_subtract_fusion
  10.7 1.2 %sort.17 = (s32[4,4,2]{0,2,1:T(2,128)}, s32[4,4,2]{0,2,1:T(2,128)S(1)}) sort(s32[4,4,2]{0,2,1:T(2,128)S(1)} %bitcast.23, s32[4,4,2]{0,2,1:T(2,128)S(1)} %iota.13), dimensions={2}, to_apply=%region_0.0 | sort | flops 160 | bytes 512 | tf_op jit(solution)/shard_map/jit(argsort)/sort | solution.py:33
  11.9 0.1 copy.7
  12.0 1.0 %reshape.42 = bf16[4,128,2,128]{3,2,1,0:T(2,128)(2,1)S(1)} reshape(bf16[512,256]{1,0:T(8,128)(2,1)} %param.4) | data formatting | bytes 524288 | tf_op jit(solution)/shard_map/reshape | solution.py:12
  13.1 0.1 fusion.5
  13.1 0.5 fusion
  13.6 0.2 copy.12
  13.8 8.6 %all-gather = bf16[4,128,512]{1,2,0:T(8,128)(2,1)S(1)} all-gather(bf16[4,128,128]{1,2,0:T(8,128)(2,1)S(1)} %bitcast.22), channel_id=2, replica_groups=mesh['row'=4,'col'=8] {'row'}, dimensions={2}, use_global_device_ids=true | all-gather | bytes 655360 | tf_op jit(solution)/shard_map/all_gather | solution.py:42
  22.4 0.3 copy.10
  22.8 0.1 fusion.3
  22.8 1.1 %multiply_bitcast_fusion = bf16[4,128,4,2,128]{4,3,2,1,0:T(2,128)(2,1)S(1)} fusion(bf16[4,4,128,128]{3,1,2,0:T(4,128)(2,1)S(1)} %copy.10, bf16[4,4,2]{2,1,0:T(4,128)(2,1)S(1)} %fusion.3), kind=kLoop, calls=%fused_computation.2 | loop fusion | flops 524288 | bytes 1572928 | tf_op jit(solution)/shard_map/idrsn,irsk->idrkn/transpose | solution.py:44
  24.0 0.8 reshape.43
  24.7 36.8 %all-gather.3.cloned.1.call-done = bf16[1024,1024]{1,0:T(8,128)(2,1)} async-done(((bf16[128,1024]{1,0:T(8,128)(2,1)}), bf16[1024,1024]{1,0:T(8,128)(2,1)}) %all-gather.3.cloned.1.call-update) | async-done | bytes 2097168 | tf_op jit(solution)/shard_map/all_gather | solution.py:59
  61.5 2.8 %multiply_reduce_fusion = (f32[1024]{0:T(1024)S(1)}, f32[512,1024]{1,0:T(8,128)S(1)}) fusion(bf16[512,1024]{1,0:T(8,128)(2,1)S(1)} %reshape.43, bf16[1024,1024]{1,0:T(8,128)(2,1)} %all-gather.3.cloned.1.call-done), kind=kOutput, calls=%fused_computation.1 | convolution fusion | flops 1074789376 | bytes 5246976 | tf_op jit(solution)/shard_map/dot_general | solution.py:57
  64.4 18.9 %psum.7 = f32[1024]{0:T(1024)S(1)} all-reduce(f32[1024]{0:T(1024)S(1)} %get-tuple-element.7), channel_id=1, replica_groups=mesh['row'=4,'col'=8] {'col'}, use_global_device_ids=true, to_apply=%region_2.3 | all-reduce | flops 1024 | bytes 8192 | tf_op jit(solution)/shard_map/psum | solution.py:63
  83.3 1.6 %multiply_divide_fusion = f32[512,1024]{1,0:T(8,128)} fusion(f32[512,1024]{1,0:T(8,128)S(1)} %get-tuple-element.8, f32[1024]{0:T(1024)S(1)} %broadcast_multiply_fusion.1), kind=kLoop, calls=%fused_computation | loop fusion | flops 1048576 | bytes 4198400 | tf_op jit(solution)/shard_map/div | solution.py:65
  (4 shorter events, 0.0 us)
Async XLA Ops:
  6.5 55.0 %all-gather.3.cloned.1.call-start = ((), (), s32[]{:S(2)}) async-start(), calls=%async_computation | async-start | bytes 2359296 | tf_op jit(solution)/shard_map/all_gather | solution.py:59
Sparse Core Ops, SparseCore 0:
  9.5 51.9 all-gather.2
where the time goes:
time: 92.1 us; the launch traced here: 91.8 us
  waiting for transfers between devices  36.8 us (40%)
  blocking collectives  27.6 us (30%)
  between operations  13.4 us (15%)
  other arithmetic  8.05 us (9%)
  matrix products  3.34 us (4%)
  local copies, waits for them, and re-layouts  2.53 us (3%)
    all_gather x1, waiting for transfers between devices, shards(): lax.all_gather(masked_right, 'col', axis=0, tiled=True)  36.8 us
    psum x1, blocking collectives, shards(): totals = lax.psum(jnp.sum(inflated, axis=0), 'col')  18.9 us
    all_gather x1, blocking collectives, shards(): gathered_left = lax.all_gather(packed_left, 'row', axis=2, tiled=True)  8.65 us
    dot_general x1, matrix products, shards(): jnp.dot(whole_left, lax.all_gather(masked_right, 'col', axis=0, tiled=Tru...  2.85 us
    mul x2, other arithmetic, expand(): masked = shaped * pattern.astype(values.dtype)[:, None, :, None]  2.43 us
  transfers between devices with their start and end apart: 1, of which 1 were waited for; matrix products, arithmetic and copies ran while one was open for 8% of the time, Pallas kernels for 0%

commit v1 on v0

v1 whole, which is shorter than its diff:
```python
import functools

import jax
import jax.numpy as jnp
from jax import lax
from jax.experimental import pallas as pl
from jax.experimental.pallas import tpu as pltpu
from jax.sharding import PartitionSpec as P

BLOCK = 128
MESH = pl.DeviceIdType.MESH


class Gather:
    def __init__(self, axis, outer, inner, held, send_sem, recv_sem):
        self.axis, self.outer, self.inner = axis, outer, inner
        self.held, self.send_sem, self.recv_sem = held, send_sem, recv_sem
        me = lax.axis_index(axis)
        self.me, self.o, self.i = me, me // inner, me % inner

    def copy(self, slot, lane, target):
        return pltpu.make_async_remote_copy(
            src_ref=self.held.at[slot],
            dst_ref=self.held.at[slot],
            send_sem=self.send_sem.at[lane, slot],
            recv_sem=self.recv_sem.at[slot],
            device_id={self.axis: target},
            device_id_type=MESH,
        )

    def each_outer(self, slot, step, act):
        target = self.o + step

        @pl.when((target >= 0) & (target < self.outer))
        def _():
            act(self.copy(slot, 0 if step == 1 else 1, target * self.inner + self.i))

    def each_inner(self, slot, step, act):
        target = self.i + step

        @pl.when((target >= 0) & (target < self.inner))
        def _():
            act(self.copy(slot, 2 if step == 1 else 3, self.o * self.inner + target))

    def visit_own(self, act):
        for step in (1, -1):
            self.each_outer(self.me, step, act)
        for step in (1, -1):
            self.each_inner(self.me, step, act)

    def visit_outer(self, o, wait, act):
        slot = o * self.inner + self.i
        if wait:
            self.copy(slot, 0, self.me).wait_recv()

        @pl.when(o < self.o)
        def _():
            self.each_outer(slot, 1, act)

        @pl.when(o > self.o)
        def _():
            self.each_outer(slot, -1, act)

        for step in (1, -1):
            self.each_inner(slot, step, act)

    def visit_inner(self, o, wait, act):
        for distance in range(1, self.inner):
            for step in (1, -1):
                i = self.i + step * distance

                @pl.when((i >= 0) & (i < self.inner))
                def _():
                    slot = o * self.inner + i
                    if wait:
                        self.copy(slot, 0, self.me).wait_recv()
                    self.each_inner(slot, -step, act)

    def place(self, q):
        distance = (q + 1) // 2
        sign = 2 * (q % 2) - 1
        o = self.o + sign * distance
        return o, (o >= 0) & (o < self.outer)


def start(copy):
    copy.start()


def wait_send(copy):
    copy.wait_send()


def kernel(
    sizes,
    left_pattern, right_pattern, left_values, right_values,
    product, scale,
    left_in, right_in, left_held, right_held, left_dense, sums,
    in_sem, left_send, left_recv, right_send, right_recv, sum_send, sum_recv,
):
    row_count, col_count, y_size, x_size = sizes
    rows_local, inner_local = left_in.shape
    left_blocks = rows_local // BLOCK
    group = inner_local // BLOCK
    left_slots = left_held.shape[2]
    col_blocks = right_in.shape[1] // BLOCK
    slots = right_held.shape[1]
    z_size = col_count // x_size
    row, col = lax.axis_index("row"), lax.axis_index("col")

    barrier = pltpu.get_barrier_semaphore()

    @pl.loop(1, col_count)
    def _(d):
        pl.semaphore_signal(
            barrier, inc=1, device_id={"col": (col + d) % col_count}, device_id_type=MESH
        )

    @pl.loop(1, row_count)
    def _(d):
        pl.semaphore_signal(
            barrier, inc=1, device_id={"row": (row + d) % row_count}, device_id_type=MESH
        )

    right_load = pltpu.make_async_copy(right_values, right_in, in_sem.at[0])
    left_load = pltpu.make_async_copy(left_values, left_in, in_sem.at[1])
    right_load.start()
    left_load.start()

    def pick(ones, wanted, candidate):
        before, found = 0, [None] * wanted
        for k, one in enumerate(ones):
            block = candidate(k)
            for s in range(min(k + 1, wanted)):
                if k == s:
                    found[s] = block
                else:
                    found[s] = jnp.where((one != 0) & (before == s), block, found[s])
            before = before + one
        return found

    def unpick(one, before, packed):
        block = jnp.zeros_like(packed[0])
        for s, value in enumerate(packed):
            block = jnp.where((one != 0) & (before == s), value, block)
        return block

    right = Gather("col", z_size, x_size, right_held, right_send, right_recv)
    left = Gather("row", y_size, row_count // y_size, left_held, left_send, left_recv)

    ones = [right_pattern[col, row * col_blocks + j] for j in range(col_blocks)]
    right_load.wait()
    picks = pick(ones, slots, lambda j: right_in[:, j * BLOCK:(j + 1) * BLOCK])
    for s in range(slots):
        right_held[col, s] = picks[s]
    pl.semaphore_wait(barrier, col_count - 1 + row_count - 1)
    right.visit_own(start)

    left_load.wait()
    for b in range(left_blocks):
        ones = [left_pattern[col * left_blocks + b, row * group + k] for k in range(group)]
        at = slice(b * BLOCK, (b + 1) * BLOCK)
        picks = pick(ones, left_slots, lambda k: left_in[at, k * BLOCK:(k + 1) * BLOCK])
        for s in range(left_slots):
            left_held[row, b, s] = picks[s]
    left.visit_own(start)

    product[...] = jnp.zeros_like(product)

    @pl.loop(1, 2 * y_size - 1)
    def _(q):
        o, valid = left.place(q)

        @pl.when(valid)
        def _():
            left.visit_outer(o, True, start)

    @pl.loop(0, y_size)
    def _(o):
        left.visit_inner(o, True, start)

    @pl.loop(0, row_count * group)
    def _(k):
        g, within = k // group, k % group
        at = pl.ds(pl.multiple_of((k % x_size) * BLOCK, BLOCK), BLOCK)
        for b in range(left_blocks):
            block_row = col * left_blocks + b
            here = left_pattern[block_row, k]
            before = 0
            for m in range(group - 1):
                before = before + jnp.where(m < within, left_pattern[block_row, g * group + m], 0)
            left_dense[k // x_size, b * BLOCK:(b + 1) * BLOCK, at] = unpick(
                here, before, [left_held[g, b, s] for s in range(left_slots)]
            )

    def multiply(o):
        right.visit_inner(o, True, start)
        ones, ranks = [], []
        for i in range(x_size):
            k = o * x_size + i
            line = [right_pattern[k, row * col_blocks + j] for j in range(col_blocks)]
            rank = [0] * col_blocks
            for j in range(1, col_blocks):
                rank[j] = rank[j - 1] + line[j - 1]
            ones.append(line)
            ranks.append(rank)

        def dense(i, j):
            packed = [right_held[o * x_size + i, s] for s in range(slots)]
            return unpick(ones[i][j], ranks[i][j], packed)

        for j in range(0, col_blocks, 2):
            block = jnp.concatenate(
                [jnp.concatenate([dense(i, j), dense(i, j + 1)], axis=1) for i in range(x_size)],
                axis=0,
            )
            at = pl.ds(j * BLOCK, 2 * BLOCK)
            product[:, at] += jnp.dot(left_dense[o], block, preferred_element_type=jnp.float32)

    @pl.loop(0, 2 * z_size - 1 + 2)
    def _(q):
        o, valid = right.place(q)

        @pl.when((q > 0) & valid)
        def _():
            right.visit_outer(o, True, start)

        late, late_valid = right.place(jnp.maximum(q - 2, 0))

        @pl.when((q >= 2) & late_valid)
        def _():
            multiply(late)

    for j in range(col_blocks):
        part = product[:, j * BLOCK:(j + 1) * BLOCK]
        sums[col, j:j + 1, :] = jnp.sum(part * part, axis=0, keepdims=True)

    def sum_copy(d):
        return pltpu.make_async_remote_copy(
            src_ref=sums.at[col],
            dst_ref=sums.at[col],
            send_sem=sum_send.at[d],
            recv_sem=sum_recv.at[col],
            device_id={"col": (col + d) % col_count},
            device_id_type=MESH,
        )

    @pl.loop(1, col_count)
    def _(d):
        sum_copy(d).start()

    right.visit_own(wait_send)
    left.visit_own(wait_send)

    @pl.loop(1, 2 * y_size - 1)
    def _(q):
        o, valid = left.place(q)

        @pl.when(valid)
        def _():
            left.visit_outer(o, False, wait_send)

    @pl.loop(0, y_size)
    def _(o):
        left.visit_inner(o, False, wait_send)

    @pl.loop(1, 2 * z_size - 1)
    def _(q):
        o, valid = right.place(q)

        @pl.when(valid)
        def _():
            right.visit_outer(o, False, wait_send)

    @pl.loop(0, z_size)
    def _(o):
        right.visit_inner(o, False, wait_send)

    @pl.loop(1, col_count)
    def _(d):
        sum_copy(d).wait_send()
        source = (col + d) % col_count
        pltpu.make_async_remote_copy(
            src_ref=sums.at[source],
            dst_ref=sums.at[source],
            send_sem=sum_send.at[d],
            recv_sem=sum_recv.at[source],
            device_id={"col": source},
            device_id_type=MESH,
        ).wait_recv()

    total = sums[0]
    for c in range(1, col_count):
        total = total + sums[c]
    factor = (rows_local * col_count) / total
    for j in range(col_blocks):
        scale[0:1, j * BLOCK:(j + 1) * BLOCK] = factor[j:j + 1, :]


def shards(row_count, col_count, left_values, left_pattern, right_values, right_pattern):
    rows_local, inner_local = left_values.shape
    inner_rows, cols_local = right_values.shape
    y_size = row_count // 2
    x_size = y_size if col_count % y_size == 0 else 1
    group = inner_local // BLOCK
    left_slots = max(1, group // 2)
    left_blocks = rows_local // BLOCK
    col_blocks = cols_local // BLOCK
    slots = col_blocks // 2
    inner = row_count * inner_local
    dma = pltpu.SemaphoreType.DMA
    product, scale = pl.pallas_call(
        functools.partial(kernel, (row_count, col_count, y_size, x_size)),
        out_shape=(
            jax.ShapeDtypeStruct((rows_local, cols_local), jnp.float32),
            jax.ShapeDtypeStruct((1, cols_local), jnp.float32),
        ),
        in_specs=[pl.BlockSpec(memory_space=pltpu.SMEM)] * 2 + [pl.BlockSpec(memory_space=pl.ANY)] * 2,
        out_specs=(pl.BlockSpec(memory_space=pltpu.VMEM),) * 2,
        scratch_shapes=[
            pltpu.VMEM((rows_local, inner_local), jnp.bfloat16),
            pltpu.VMEM((inner_rows, cols_local), jnp.bfloat16),
            pltpu.VMEM((row_count, left_blocks, left_slots, BLOCK, BLOCK), jnp.bfloat16),
            pltpu.VMEM((col_count, slots, BLOCK, BLOCK), jnp.bfloat16),
            pltpu.VMEM((inner // (x_size * BLOCK), rows_local, x_size * BLOCK), jnp.bfloat16),
            pltpu.VMEM((col_count, col_blocks, BLOCK), jnp.float32),
            dma((2,)),
            dma((4, row_count)),
            dma((row_count,)),
            dma((4, col_count)),
            dma((col_count,)),
            dma((col_count,)),
            dma((col_count,)),
        ],
        compiler_params=pltpu.CompilerParams(
            collective_id=0, has_side_effects=True, vmem_limit_bytes=32 * 1024 * 1024
        ),
    )(left_pattern, right_pattern, left_values, right_values)
    return product * product * scale


def solution(mesh):
    return jax.shard_map(
        functools.partial(shards, mesh.shape["row"], mesh.shape["col"]),
        mesh=mesh,
        in_specs=(P("col", "row"), P(), P("col", "row"), P()),
        out_specs=P("col", "row"),
        check_vma=False,
    )
```

time: 92.1 us -> 37.1 us (0.40)
  waiting for transfers between devices: 36.8 us -> 0 us
  Pallas kernels: 0 us -> 31.9 us
  blocking collectives: 27.6 us -> 0 us
  between operations: 13.4 us -> 0.01 us
  other arithmetic: 8.05 us -> 1.57 us
  matrix products: 3.34 us -> 0 us
    all_gather x1 -> x0, waiting for transfers between devices: 36.8 us -> none  [shards(): lax.all_gather(masked_right, 'col', axis=0, tiled=True)]
    pallas_call x0 -> x1, Pallas kernels: none -> 31.9 us  [shards(): pl.pallas_call(functools.partial(kernel, (row_count, col_count, y_size, x...]
    psum x1 -> x0, blocking collectives: 18.9 us -> none  [shards(): totals = lax.psum(jnp.sum(inflated, axis=0), 'col')]
    all_gather x1 -> x0, blocking collectives: 8.65 us -> none  [shards(): gathered_left = lax.all_gather(packed_left, 'row', axis=2, tiled=True)]
    unnamed x0 -> x7, local copies, waits for them, and re-layouts: none -> 3.35 us
    dot_general x2 -> x0, matrix products: 3.34 us -> none  [the longest x1 2.85 us: shards(): jnp.dot(whole_left, lax.all_gather(masked_right, 'col', axis=0, tiled=Tru...]
    reshape x2 -> x0, local copies, waits for them, and re-layouts: 1.78 us -> none  [the longest x1 1.02 us: expand(): values.reshape(block_rows, height // block_rows, block_cols, width // blo...]
    div x2 -> x0, other arithmetic: 1.61 us -> none  [the longest x1 1.6 us: shards(): return inflated / column_mean[None, :]]
  transfers between devices with their start and end apart: 1 -> 0, of which waited for: 1 -> 0; matrix products, arithmetic and copies ran while one was open for 8% -> 0% of each run, Pallas kernels for 0% -> 0%
where the time goes in v1:
time: 37.1 us; the launch traced here: 36.9 us
  Pallas kernels  31.9 us (86%)
  local copies, waits for them, and re-layouts  3.35 us (9%)
  other arithmetic  1.57 us (4%)
    pallas_call x1, Pallas kernels, shards(): pl.pallas_call(functools.partial(kernel, (row_count, col_count, y_size, x...  31.9 us
    unnamed x7, local copies, waits for them, and re-layouts  3.35 us
    mul x1, other arithmetic, shards(): return product * product * scale  1.57 us

profile of v1, /device:TPU:0, one launch (start us, length us, event | category | flops | bytes accessed | tf_op | source)
XLA Modules:
  0.0 36.9 jit_solution(2442856668803982413)
XLA Ops:
  0.0 0.8 %copy.5.left_pattern = s32[32,8]{1,0:T(8,128)S(1)} copy(s32[32,8]{0,1:T(8,128)} %param.5) | data formatting | bytes 2048 | tf_op args[1]
  0.8 0.0 copy-start
  0.8 0.9 %copy-done = bf16[512,256]{1,0:T(8,128)(2,1)S(1)} copy-done((bf16[512,256]{1,0:T(8,128)(2,1)S(1)}, bf16[512,256]{1,0:T(8,128)(2,1)}, u32[]{:S(2)}) %copy-start) | copy-done | bytes 262168
  1.7 0.0 copy-start.1
  1.7 0.9 %copy-done.1 = bf16[128,1024]{1,0:T(8,128)(2,1)S(1)} copy-done((bf16[128,1024]{1,0:T(8,128)(2,1)S(1)}, bf16[128,1024]{1,0:T(8,128)(2,1)}, u32[]{:S(2)}) %copy-start.1) | copy-done | bytes 262168
  2.7 0.0 copy-start.2
  2.7 0.7 %copy-done.2 = s32[8,32]{1,0:T(8,128)S(1)} copy-done((s32[8,32]{1,0:T(8,128)S(1)}, s32[8,32]{1,0:T(8,128)}, u32[]{:S(2)}) %copy-start.2) | copy-done | bytes 1048
  3.4 31.9 %shard_map.46 = (f32[512,1024]{1,0:T(8,128)S(1)}, f32[1,1024]{1,0:T(1,128)S(1)}) custom-call(s32[32,8]{1,0:T(8,128)S(1)} %copy.5.left_pattern, s32[8,32]{1,0:T(8,128)S(1)} %copy-done.2, bf16[512,256]{1,0:T(8,128)(2,1)S(1)} %copy-done, bf16[128,1024]{1,0:T(8,128)(2,1)S(1)} %copy-done.1), custom_call_target="tpu_custom_call" | custom-call | tf_op jit(solution)/shard_map/pallas_call | solution.py:312
  35.3 1.6 %multiply_multiply_fusion = f32[512,1024]{1,0:T(8,128)} fusion(f32[512,1024]{1,0:T(8,128)S(1)} %get-tuple-element.7, f32[1024]{0:T(1024)S(1)} %bitcast.1), kind=kLoop, calls=%fused_computation | loop fusion | flops 1048576 | bytes 4198400 | tf_op jit(solution)/shard_map/mul | solution.py:339
Async XLA Ops:
  0.8 0.9 %copy-start = (bf16[512,256]{1,0:T(8,128)(2,1)S(1)}, bf16[512,256]{1,0:T(8,128)(2,1)}, u32[]{:S(2)}) copy-start(bf16[512,256]{1,0:T(8,128)(2,1)} %left_values.1) | copy-start | bytes 786436
  1.7 0.9 %copy-start.1 = (bf16[128,1024]{1,0:T(8,128)(2,1)S(1)}, bf16[128,1024]{1,0:T(8,128)(2,1)}, u32[]{:S(2)}) copy-start(bf16[128,1024]{1,0:T(8,128)(2,1)} %right_values.1) | copy-start | bytes 786436
  2.7 0.7 %copy-start.2 = (s32[8,32]{1,0:T(8,128)S(1)}, s32[8,32]{1,0:T(8,128)}, u32[]{:S(2)}) copy-start(s32[8,32]{1,0:T(8,128)} %right_pattern.1) | copy-start | bytes 3076

commit v2 on v1

--- a/solution.py
+++ b/solution.py
@@ -15,54 +15,59 @@
     def __init__(self, axis, outer, inner, held, send_sem, recv_sem):
         self.axis, self.outer, self.inner = axis, outer, inner
         self.held, self.send_sem, self.recv_sem = held, send_sem, recv_sem
+        self.parts = recv_sem.shape[1]
+        self.depth = held.shape[1] // self.parts
         me = lax.axis_index(axis)
         self.me, self.o, self.i = me, me // inner, me % inner
 
-    def copy(self, slot, lane, target):
+    def copy(self, slot, part, lane, target):
+        piece = self.held.at[slot, pl.ds(part * self.depth, self.depth)]
         return pltpu.make_async_remote_copy(
-            src_ref=self.held.at[slot],
-            dst_ref=self.held.at[slot],
-            send_sem=self.send_sem.at[lane, slot],
-            recv_sem=self.recv_sem.at[slot],
+            src_ref=piece,
+            dst_ref=piece,
+            send_sem=self.send_sem.at[lane, slot, part],
+            recv_sem=self.recv_sem.at[slot, part],
             device_id={self.axis: target},
             device_id_type=MESH,
         )
 
-    def each_outer(self, slot, step, act):
+    def each_outer(self, slot, part, step, act):
         target = self.o + step
 
         @pl.when((target >= 0) & (target < self.outer))
         def _():
-            act(self.copy(slot, 0 if step == 1 else 1, target * self.inner + self.i))
-
-    def each_inner(self, slot, step, act):
+            act(self.copy(slot, part, 0 if step == 1 else 1, target * self.inner + self.i))
+
+    def each_inner(self, slot, part, step, act):
         target = self.i + step
 
         @pl.when((target >= 0) & (target < self.inner))
         def _():
-            act(self.copy(slot, 2 if step == 1 else 3, self.o * self.inner + target))
+            act(self.copy(slot, part, 2 if step == 1 else 3, self.o * self.inner + target))
 
     def visit_own(self, act):
-        for step in (1, -1):
-            self.each_outer(self.me, step, act)
-        for step in (1, -1):
-            self.each_inner(self.me, step, act)
+        for part in range(self.parts):
+            for step in (1, -1):
+                self.each_outer(self.me, part, step, act)
+            for step in (1, -1):
+                self.each_inner(self.me, part, step, act)
 
     def visit_outer(self, o, wait, act):
         slot = o * self.inner + self.i
-        if wait:
-            self.copy(slot, 0, self.me).wait_recv()
-
-        @pl.when(o < self.o)
-        def _():
-            self.each_outer(slot, 1, act)
-
-        @pl.when(o > self.o)
-        def _():
-            self.each_outer(slot, -1, act)
-
-        for step in (1, -1):
-            self.each_inner(slot, step, act)
+        for part in range(self.parts):
+            if wait:
+                self.copy(slot, part, 0, self.me).wait_recv()
+
+            @pl.when(o < self.o)
+            def _():
+                self.each_outer(slot, part, 1, act)
+
+            @pl.when(o > self.o)
+            def _():
+                self.each_outer(slot, part, -1, act)
+
+            for step in (1, -1):
+                self.each_inner(slot, part, step, act)
 
     def visit_inner(self, o, wait, act):
         for distance in range(1, self.inner):
@@ -72,9 +77,10 @@
                 @pl.when((i >= 0) & (i < self.inner))
                 def _():
                     slot = o * self.inner + i
-                    if wait:
-                        self.copy(slot, 0, self.me).wait_recv()
-                    self.each_inner(slot, -step, act)
+                    for part in range(self.parts):
+                        if wait:
+                            self.copy(slot, part, 0, self.me).wait_recv()
+                        self.each_inner(slot, part, -step, act)
 
     def place(self, q):
         distance = (q + 1) // 2
@@ -93,9 +99,9 @@
 
 def kernel(
     sizes,
-    left_pattern, right_pattern, left_values, right_values,
+    left_ones, right_ones, left_values, right_values,
     product, scale,
-    left_in, right_in, left_held, right_held, left_dense, sums,
+    left_pattern, right_pattern, left_in, right_in, left_held, right_held, left_dense, sums,
     in_sem, left_send, left_recv, right_send, right_recv, sum_send, sum_recv,
 ):
     row_count, col_count, y_size, x_size = sizes
@@ -124,7 +130,11 @@
 
     right_load = pltpu.make_async_copy(right_values, right_in, in_sem.at[0])
     left_load = pltpu.make_async_copy(left_values, left_in, in_sem.at[1])
+    left_ones_load = pltpu.make_async_copy(left_ones, left_pattern, in_sem.at[2])
+    right_ones_load = pltpu.make_async_copy(right_ones, right_pattern, in_sem.at[3])
+    right_ones_load.start()
     right_load.start()
+    left_ones_load.start()
     left_load.start()
 
     def pick(ones, wanted, candidate):
@@ -148,6 +158,7 @@
     right = Gather("col", z_size, x_size, right_held, right_send, right_recv)
     left = Gather("row", y_size, row_count // y_size, left_held, left_send, left_recv)
 
+    right_ones_load.wait()
     ones = [right_pattern[col, row * col_blocks + j] for j in range(col_blocks)]
     right_load.wait()
     picks = pick(ones, slots, lambda j: right_in[:, j * BLOCK:(j + 1) * BLOCK])
@@ -156,9 +167,10 @@
     pl.semaphore_wait(barrier, col_count - 1 + row_count - 1)
     right.visit_own(start)
 
+    left_ones_load.wait()
     left_load.wait()
     for b in range(left_blocks):
-        ones = [left_pattern[col * left_blocks + b, row * group + k] for k in range(group)]
+        ones = [left_pattern[row * group + k, col * left_blocks + b] for k in range(group)]
         at = slice(b * BLOCK, (b + 1) * BLOCK)
         picks = pick(ones, left_slots, lambda k: left_in[at, k * BLOCK:(k + 1) * BLOCK])
         for s in range(left_slots):
@@ -185,10 +197,10 @@
         at = pl.ds(pl.multiple_of((k % x_size) * BLOCK, BLOCK), BLOCK)
         for b in range(left_blocks):
             block_row = col * left_blocks + b
-            here = left_pattern[block_row, k]
+            here = left_pattern[k, block_row]
             before = 0
             for m in range(group - 1):
-                before = before + jnp.where(m < within, left_pattern[block_row, g * group + m], 0)
+                before = before + jnp.where(m < within, left_pattern[g * group + m, block_row], 0)
             left_dense[k // x_size, b * BLOCK:(b + 1) * BLOCK, at] = unpick(
                 here, before, [left_held[g, b, s] for s in range(left_slots)]
             )
@@ -307,35 +319,39 @@
     left_blocks = rows_local // BLOCK
     col_blocks = cols_local // BLOCK
     slots = col_blocks // 2
+    parts = 2
     inner = row_count * inner_local
     dma = pltpu.SemaphoreType.DMA
+    operands = (left_pattern.T, right_pattern, left_values, right_values)
     product, scale = pl.pallas_call(
         functools.partial(kernel, (row_count, col_count, y_size, x_size)),
         out_shape=(
             jax.ShapeDtypeStruct((rows_local, cols_local), jnp.float32),
             jax.ShapeDtypeStruct((1, cols_local), jnp.float32),
         ),
-        in_specs=[pl.BlockSpec(memory_space=pltpu.SMEM)] * 2 + [pl.BlockSpec(memory_space=pl.ANY)] * 2,
+        in_specs=[pl.BlockSpec(memory_space=pltpu.HBM)] * 4,
         out_specs=(pl.BlockSpec(memory_space=pltpu.VMEM),) * 2,
         scratch_shapes=[
+            pltpu.SMEM(left_pattern.shape[::-1], jnp.int32),
+            pltpu.SMEM(right_pattern.shape, jnp.int32),
             pltpu.VMEM((rows_local, inner_local), jnp.bfloat16),
             pltpu.VMEM((inner_rows, cols_local), jnp.bfloat16),
             pltpu.VMEM((row_count, left_blocks, left_slots, BLOCK, BLOCK), jnp.bfloat16),
             pltpu.VMEM((col_count, slots, BLOCK, BLOCK), jnp.bfloat16),
             pltpu.VMEM((inner // (x_size * BLOCK), rows_local, x_size * BLOCK), jnp.bfloat16),
             pltpu.VMEM((col_count, col_blocks, BLOCK), jnp.float32),
-            dma((2,)),
-            dma((4, row_count)),
-            dma((row_count,)),
-            dma((4, col_count)),
-            dma((col_count,)),
+            dma((4,)),
+            dma((4, row_count, 1)),
+            dma((row_count, 1)),
+            dma((4, col_count, parts)),
+            dma((col_count, parts)),
             dma((col_count,)),
             dma((col_count,)),
         ],
         compiler_params=pltpu.CompilerParams(
             collective_id=0, has_side_effects=True, vmem_limit_bytes=32 * 1024 * 1024
         ),
-    )(left_pattern, right_pattern, left_values, right_values)
+    )(*(pltpu.with_memory_space_constraint(x, pltpu.HBM) for x in operands))
     return product * product * scale
 
 

time: 37.1 us -> 31.5 us (0.85)
  local copies, waits for them, and re-layouts: 3.35 us -> 0 us
  Pallas kernels: 31.9 us -> 29.6 us
    unnamed x7 -> x0, local copies, waits for them, and re-layouts: 3.35 us -> none
    pallas_call x1, Pallas kernels: 31.9 us -> 29.6 us  [shards(): pl.pallas_call(functools.partial(kernel, (row_count, col_count, y_size, x...]
where the time goes in v2:
time: 31.5 us; the launch traced here: 31.3 us
  Pallas kernels  29.6 us (94%)
  other arithmetic  1.71 us (5%)
    pallas_call x1, Pallas kernels, shards(): pl.pallas_call(functools.partial(kernel, (row_count, col_count, y_size, x...  29.6 us
    mul x1, other arithmetic, shards(): return product * product * scale  1.71 us

profile of v2, /device:TPU:0, one launch (start us, length us, event | category | flops | bytes accessed | tf_op | source)
XLA Modules:
  0.0 31.3 jit_solution(4823917771633738036)
XLA Ops:
  0.0 29.6 %shard_map.46 = (f32[512,1024]{1,0:T(8,128)S(1)}, f32[1,1024]{1,0:T(1,128)S(1)}) custom-call(s32[8,32]{1,0:T(8,128)} %bitcast.3, s32[8,32]{1,0:T(8,128)} %right_ones.1, bf16[512,256]{1,0:T(8,128)(2,1)} %left_values.1, bf16[128,1024]{1,0:T(8,128)(2,1)} %right_values.1), custom_call_target="tpu_custom_call" | custom-call | tf_op jit(solution)/shard_map/pallas_call | solution.py:326
  29.6 1.7 %multiply_multiply_fusion = f32[512,1024]{1,0:T(8,128)} fusion(f32[512,1024]{1,0:T(8,128)S(1)} %get-tuple-element.7, f32[1024]{0:T(1024)S(1)} %bitcast.2), kind=kLoop, calls=%fused_computation | loop fusion | flops 1048576 | bytes 4198400 | tf_op jit(solution)/shard_map/mul | solution.py:355

commit v3 on v2

--- a/solution.py
+++ b/solution.py
@@ -83,10 +83,23 @@
                         self.each_inner(slot, part, -step, act)
 
     def place(self, q):
-        distance = (q + 1) // 2
-        sign = 2 * (q % 2) - 1
-        o = self.o + sign * distance
+        o = jnp.where(q < self.outer, self.o - q, self.o + q - self.outer + 1)
         return o, (o >= 0) & (o < self.outer)
+
+    def greet(self, barrier):
+        count = 0
+        for step in (1, -1):
+            for own, size, stride in ((self.o, self.outer, self.inner), (self.i, self.inner, 1)):
+                there = (own + step >= 0) & (own + step < size)
+
+                @pl.when(there)
+                def _():
+                    pl.semaphore_signal(
+                        barrier, inc=1, device_id={self.axis: self.me + step * stride}, device_id_type=MESH
+                    )
+
+                count = count + jnp.where(there, 1, 0)
+        return count
 
 
 def start(copy):
@@ -116,17 +129,9 @@
 
     barrier = pltpu.get_barrier_semaphore()
 
-    @pl.loop(1, col_count)
-    def _(d):
-        pl.semaphore_signal(
-            barrier, inc=1, device_id={"col": (col + d) % col_count}, device_id_type=MESH
-        )
-
-    @pl.loop(1, row_count)
-    def _(d):
-        pl.semaphore_signal(
-            barrier, inc=1, device_id={"row": (row + d) % row_count}, device_id_type=MESH
-        )
+    right = Gather("col", z_size, x_size, right_held, right_send, right_recv)
+    left = Gather("row", y_size, row_count // y_size, left_held, left_send, left_recv)
+    neighbours = right.greet(barrier) + left.greet(barrier)
 
     right_load = pltpu.make_async_copy(right_values, right_in, in_sem.at[0])
     left_load = pltpu.make_async_copy(left_values, left_in, in_sem.at[1])
@@ -155,16 +160,13 @@
             block = jnp.where((one != 0) & (before == s), value, block)
         return block
 
-    right = Gather("col", z_size, x_size, right_held, right_send, right_recv)
-    left = Gather("row", y_size, row_count // y_size, left_held, left_send, left_recv)
-
     right_ones_load.wait()
     ones = [right_pattern[col, row * col_blocks + j] for j in range(col_blocks)]
     right_load.wait()
     picks = pick(ones, slots, lambda j: right_in[:, j * BLOCK:(j + 1) * BLOCK])
     for s in range(slots):
         right_held[col, s] = picks[s]
-    pl.semaphore_wait(barrier, col_count - 1 + row_count - 1)
+    pl.semaphore_wait(barrier, neighbours)
     right.visit_own(start)
 
     left_ones_load.wait()
@@ -179,31 +181,32 @@
 
     product[...] = jnp.zeros_like(product)
 
-    @pl.loop(1, 2 * y_size - 1)
-    def _(q):
-        o, valid = left.place(q)
-
-        @pl.when(valid)
-        def _():
-            left.visit_outer(o, True, start)
-
-    @pl.loop(0, y_size)
-    def _(o):
-        left.visit_inner(o, True, start)
-
-    @pl.loop(0, row_count * group)
-    def _(k):
-        g, within = k // group, k % group
-        at = pl.ds(pl.multiple_of((k % x_size) * BLOCK, BLOCK), BLOCK)
-        for b in range(left_blocks):
-            block_row = col * left_blocks + b
-            here = left_pattern[k, block_row]
-            before = 0
-            for m in range(group - 1):
-                before = before + jnp.where(m < within, left_pattern[g * group + m, block_row], 0)
-            left_dense[k // x_size, b * BLOCK:(b + 1) * BLOCK, at] = unpick(
-                here, before, [left_held[g, b, s] for s in range(left_slots)]
-            )
+    def finish_left():
+        @pl.loop(1, 2 * y_size - 1)
+        def _(q):
+            o, valid = left.place(q)
+
+            @pl.when(valid)
+            def _():
+                left.visit_outer(o, True, start)
+
+        @pl.loop(0, y_size)
+        def _(o):
+            left.visit_inner(o, True, start)
+
+        @pl.loop(0, row_count * group)
+        def _(k):
+            g, within = k // group, k % group
+            at = pl.ds(pl.multiple_of((k % x_size) * BLOCK, BLOCK), BLOCK)
+            for b in range(left_blocks):
+                block_row = col * left_blocks + b
+                here = left_pattern[k, block_row]
+                before = 0
+                for m in range(group - 1):
+                    before = before + jnp.where(m < within, left_pattern[g * group + m, block_row], 0)
+                left_dense[k // x_size, b * BLOCK:(b + 1) * BLOCK, at] = unpick(
+                    here, before, [left_held[g, b, s] for s in range(left_slots)]
+                )
 
     def multiply(o):
         right.visit_inner(o, True, start)
@@ -229,17 +232,21 @@
             at = pl.ds(j * BLOCK, 2 * BLOCK)
             product[:, at] += jnp.dot(left_dense[o], block, preferred_element_type=jnp.float32)
 
-    @pl.loop(0, 2 * z_size - 1 + 2)
+    @pl.loop(0, 2 * z_size)
     def _(q):
         o, valid = right.place(q)
 
-        @pl.when((q > 0) & valid)
+        @pl.when((q > 0) & (q < 2 * z_size - 1) & valid)
         def _():
             right.visit_outer(o, True, start)
 
-        late, late_valid = right.place(jnp.maximum(q - 2, 0))
-
-        @pl.when((q >= 2) & late_valid)
+        @pl.when(q == 1)
+        def _():
+            finish_left()
+
+        late, late_valid = right.place(jnp.maximum(q - 1, 0))
+
+        @pl.when((q >= 1) & late_valid)
         def _():
             multiply(late)
 

time: 31.5 us -> 34.5 us (1.095)
  Pallas kernels: 29.6 us -> 32.6 us
    pallas_call x1, Pallas kernels: 29.6 us -> 32.6 us  [shards(): pl.pallas_call(functools.partial(kernel, (row_count, col_count, y_size, x...]
where the time goes in v3:
time: 34.5 us; the launch traced here: 34.4 us
  Pallas kernels  32.6 us (94%)
  other arithmetic  1.71 us (5%)
    pallas_call x1, Pallas kernels, shards(): pl.pallas_call(functools.partial(kernel, (row_count, col_count, y_size, x...  32.6 us
    mul x1, other arithmetic, shards(): return product * product * scale  1.71 us

profile of v3, /device:TPU:0, one launch (start us, length us, event | category | flops | bytes accessed | tf_op | source)
XLA Modules:
  0.0 34.4 jit_solution(2112084292214742499)
XLA Ops:
  0.0 32.6 %shard_map.46 = (f32[512,1024]{1,0:T(8,128)S(1)}, f32[1,1024]{1,0:T(1,128)S(1)}) custom-call(s32[8,32]{1,0:T(8,128)} %bitcast.3, s32[8,32]{1,0:T(8,128)} %right_ones.1, bf16[512,256]{1,0:T(8,128)(2,1)} %left_values.1, bf16[128,1024]{1,0:T(8,128)(2,1)} %right_values.1), custom_call_target="tpu_custom_call" | custom-call | tf_op jit(solution)/shard_map/pallas_call | solution.py:333
  32.6 1.7 %multiply_multiply_fusion = f32[512,1024]{1,0:T(8,128)} fusion(f32[512,1024]{1,0:T(8,128)S(1)} %get-tuple-element.7, f32[1024]{0:T(1024)S(1)} %bitcast.2), kind=kLoop, calls=%fused_computation | loop fusion | flops 1048576 | bytes 4198400 | tf_op jit(solution)/shard_map/mul | solution.py:362

commit v4 on v3

--- a/solution.py
+++ b/solution.py
@@ -12,60 +12,54 @@
 
 
 class Gather:
-    def __init__(self, axis, outer, inner, held, send_sem, recv_sem):
+    def __init__(self, axis, outer, inner, held, own_send, send_sem, recv_sem):
         self.axis, self.outer, self.inner = axis, outer, inner
-        self.held, self.send_sem, self.recv_sem = held, send_sem, recv_sem
+        self.held, self.own_send, self.send_sem, self.recv_sem = held, own_send, send_sem, recv_sem
         self.parts = recv_sem.shape[1]
         self.depth = held.shape[1] // self.parts
         me = lax.axis_index(axis)
         self.me, self.o, self.i = me, me // inner, me % inner
 
-    def copy(self, slot, part, lane, target):
+    def copy(self, slot, part, send_sem, target):
         piece = self.held.at[slot, pl.ds(part * self.depth, self.depth)]
         return pltpu.make_async_remote_copy(
             src_ref=piece,
             dst_ref=piece,
-            send_sem=self.send_sem.at[lane, slot, part],
+            send_sem=send_sem,
             recv_sem=self.recv_sem.at[slot, part],
             device_id={self.axis: target},
             device_id_type=MESH,
         )
 
-    def each_outer(self, slot, part, step, act):
-        target = self.o + step
-
-        @pl.when((target >= 0) & (target < self.outer))
-        def _():
-            act(self.copy(slot, part, 0 if step == 1 else 1, target * self.inner + self.i))
+    def wait(self, slot, part):
+        self.copy(slot, part, self.own_send.at[0, part], self.me).wait_recv()
 
     def each_inner(self, slot, part, step, act):
         target = self.i + step
 
         @pl.when((target >= 0) & (target < self.inner))
         def _():
-            act(self.copy(slot, part, 2 if step == 1 else 3, self.o * self.inner + target))
+            sem = self.send_sem.at[0 if step == 1 else 1, slot, part]
+            act(self.copy(slot, part, sem, self.o * self.inner + target))
 
     def visit_own(self, act):
         for part in range(self.parts):
             for step in (1, -1):
-                self.each_outer(self.me, part, step, act)
-            for step in (1, -1):
                 self.each_inner(self.me, part, step, act)
+            for distance in range(1, self.outer):
+                for step in (distance, -distance):
+                    target = self.o + step
+
+                    @pl.when((target >= 0) & (target < self.outer))
+                    def _():
+                        sem = self.own_send.at[target, part]
+                        act(self.copy(self.me, part, sem, target * self.inner + self.i))
 
     def visit_outer(self, o, wait, act):
         slot = o * self.inner + self.i
         for part in range(self.parts):
             if wait:
-                self.copy(slot, part, 0, self.me).wait_recv()
-
-            @pl.when(o < self.o)
-            def _():
-                self.each_outer(slot, part, 1, act)
-
-            @pl.when(o > self.o)
-            def _():
-                self.each_outer(slot, part, -1, act)
-
+                self.wait(slot, part)
             for step in (1, -1):
                 self.each_inner(slot, part, step, act)
 
@@ -79,26 +73,33 @@
                     slot = o * self.inner + i
                     for part in range(self.parts):
                         if wait:
-                            self.copy(slot, part, 0, self.me).wait_recv()
+                            self.wait(slot, part)
                         self.each_inner(slot, part, -step, act)
 
     def place(self, q):
-        o = jnp.where(q < self.outer, self.o - q, self.o + q - self.outer + 1)
+        distance = (q + 1) // 2
+        sign = 2 * (q % 2) - 1
+        o = self.o + sign * distance
         return o, (o >= 0) & (o < self.outer)
 
     def greet(self, barrier):
-        count = 0
+        count = self.outer - 1
+
+        @pl.loop(1, self.outer)
+        def _(d):
+            target = ((self.o + d) % self.outer) * self.inner + self.i
+            pl.semaphore_signal(barrier, inc=1, device_id={self.axis: target}, device_id_type=MESH)
+
         for step in (1, -1):
-            for own, size, stride in ((self.o, self.outer, self.inner), (self.i, self.inner, 1)):
-                there = (own + step >= 0) & (own + step < size)
-
-                @pl.when(there)
-                def _():
-                    pl.semaphore_signal(
-                        barrier, inc=1, device_id={self.axis: self.me + step * stride}, device_id_type=MESH
-                    )
-
-                count = count + jnp.where(there, 1, 0)
+            there = (self.i + step >= 0) & (self.i + step < self.inner)
+
+            @pl.when(there)
+            def _():
+                pl.semaphore_signal(
+                    barrier, inc=1, device_id={self.axis: self.me + step}, device_id_type=MESH
+                )
+
+            count = count + jnp.where(there, 1, 0)
         return count
 
 
@@ -115,7 +116,7 @@
     left_ones, right_ones, left_values, right_values,
     product, scale,
     left_pattern, right_pattern, left_in, right_in, left_held, right_held, left_dense, sums,
-    in_sem, left_send, left_recv, right_send, right_recv, sum_send, sum_recv,
+    in_sem, left_own, left_send, left_recv, right_own, right_send, right_recv, sum_send, sum_recv,
 ):
     row_count, col_count, y_size, x_size = sizes
     rows_local, inner_local = left_in.shape
@@ -129,8 +130,8 @@
 
     barrier = pltpu.get_barrier_semaphore()
 
-    right = Gather("col", z_size, x_size, right_held, right_send, right_recv)
-    left = Gather("row", y_size, row_count // y_size, left_held, left_send, left_recv)
+    right = Gather("col", z_size, x_size, right_held, right_own, right_send, right_recv)
+    left = Gather("row", y_size, row_count // y_size, left_held, left_own, left_send, left_recv)
     neighbours = right.greet(barrier) + left.greet(barrier)
 
     right_load = pltpu.make_async_copy(right_values, right_in, in_sem.at[0])
@@ -232,21 +233,21 @@
             at = pl.ds(j * BLOCK, 2 * BLOCK)
             product[:, at] += jnp.dot(left_dense[o], block, preferred_element_type=jnp.float32)
 
-    @pl.loop(0, 2 * z_size)
+    @pl.loop(0, 2 * z_size - 1 + 2)
     def _(q):
         o, valid = right.place(q)
 
-        @pl.when((q > 0) & (q < 2 * z_size - 1) & valid)
+        @pl.when((q > 0) & valid)
         def _():
             right.visit_outer(o, True, start)
 
-        @pl.when(q == 1)
+        @pl.when(q == 2)
         def _():
             finish_left()
 
-        late, late_valid = right.place(jnp.maximum(q - 1, 0))
-
-        @pl.when((q >= 1) & late_valid)
+        late, late_valid = right.place(jnp.maximum(q - 2, 0))
+
+        @pl.when((q >= 2) & late_valid)
         def _():
             multiply(late)
 
@@ -348,9 +349,11 @@
             pltpu.VMEM((inner // (x_size * BLOCK), rows_local, x_size * BLOCK), jnp.bfloat16),
             pltpu.VMEM((col_count, col_blocks, BLOCK), jnp.float32),
             dma((4,)),
-            dma((4, row_count, 1)),
+            dma((y_size, 1)),
+            dma((2, row_count, 1)),
             dma((row_count, 1)),
-            dma((4, col_count, parts)),
+            dma((col_count // x_size, parts)),
+            dma((2, col_count, parts)),
             dma((col_count, parts)),
             dma((col_count,)),
             dma((col_count,)),

time: 34.5 us -> 30.5 us (0.88)
  Pallas kernels: 32.6 us -> 28.6 us
    pallas_call x1, Pallas kernels: 32.6 us -> 28.6 us  [shards(): pl.pallas_call(functools.partial(kernel, (row_count, col_count, y_size, x...]
where the time goes in v4:
time: 30.5 us; the launch traced here: 30.4 us
  Pallas kernels  28.6 us (94%)
  other arithmetic  1.71 us (6%)
    pallas_call x1, Pallas kernels, shards(): pl.pallas_call(functools.partial(kernel, (row_count, col_count, y_size, x...  28.6 us
    mul x1, other arithmetic, shards(): return product * product * scale  1.71 us

profile of v4, /device:TPU:0, one launch (start us, length us, event | category | flops | bytes accessed | tf_op | source)
XLA Modules:
  0.0 30.4 jit_solution(12952322730212562298)
XLA Ops:
  0.0 28.6 %shard_map.46 = (f32[512,1024]{1,0:T(8,128)S(1)}, f32[1,1024]{1,0:T(1,128)S(1)}) custom-call(s32[8,32]{1,0:T(8,128)} %bitcast.3, s32[8,32]{1,0:T(8,128)} %right_ones.1, bf16[512,256]{1,0:T(8,128)(2,1)} %left_values.1, bf16[128,1024]{1,0:T(8,128)(2,1)} %right_values.1), custom_call_target="tpu_custom_call" | custom-call | tf_op jit(solution)/shard_map/pallas_call | solution.py:334
  28.7 1.7 %multiply_multiply_fusion = f32[512,1024]{1,0:T(8,128)} fusion(f32[512,1024]{1,0:T(8,128)S(1)} %get-tuple-element.7, f32[1024]{0:T(1024)S(1)} %bitcast.2), kind=kLoop, calls=%fused_computation | loop fusion | flops 1048576 | bytes 4198400 | tf_op jit(solution)/shard_map/mul | solution.py:365

commit v5 on v4

--- a/solution.py
+++ b/solution.py
@@ -115,15 +115,14 @@
     sizes,
     left_ones, right_ones, left_values, right_values,
     product, scale,
-    left_pattern, right_pattern, left_in, right_in, left_held, right_held, left_dense, sums,
-    in_sem, left_own, left_send, left_recv, right_own, right_send, right_recv, sum_send, sum_recv,
+    left_pattern, right_pattern, left_in, right_in, left_held, right_held, left_dense, stage, sums,
+    ones_sem, left_sem, right_sem, left_own, left_send, left_recv, right_own, right_send, right_recv, sum_send, sum_recv,
 ):
     row_count, col_count, y_size, x_size = sizes
-    rows_local, inner_local = left_in.shape
-    left_blocks = rows_local // BLOCK
-    group = inner_local // BLOCK
+    left_blocks, group = left_in.shape[:2]
+    rows_local = left_blocks * BLOCK
     left_slots = left_held.shape[2]
-    col_blocks = right_in.shape[1] // BLOCK
+    col_blocks = right_in.shape[0]
     slots = right_held.shape[1]
     z_size = col_count // x_size
     row, col = lax.axis_index("row"), lax.axis_index("col")
@@ -134,25 +133,30 @@
     left = Gather("row", y_size, row_count // y_size, left_held, left_own, left_send, left_recv)
     neighbours = right.greet(barrier) + left.greet(barrier)
 
-    right_load = pltpu.make_async_copy(right_values, right_in, in_sem.at[0])
-    left_load = pltpu.make_async_copy(left_values, left_in, in_sem.at[1])
-    left_ones_load = pltpu.make_async_copy(left_ones, left_pattern, in_sem.at[2])
-    right_ones_load = pltpu.make_async_copy(right_ones, right_pattern, in_sem.at[3])
+    left_ones_load = pltpu.make_async_copy(left_ones, left_pattern, ones_sem.at[0])
+    right_ones_load = pltpu.make_async_copy(right_ones, right_pattern, ones_sem.at[1])
+    left_ones_load.start()
     right_ones_load.start()
-    right_load.start()
-    left_ones_load.start()
-    left_load.start()
-
-    def pick(ones, wanted, candidate):
-        before, found = 0, [None] * wanted
+    loads = []
+    for b in range(left_blocks):
+        for k in range(group):
+            source = left_values.at[pl.ds(b * BLOCK, BLOCK), pl.ds(k * BLOCK, BLOCK)]
+            loads.append(pltpu.make_async_copy(source, left_in.at[b, k], left_sem.at[b, k]))
+    right_loads = []
+    for j in range(col_blocks):
+        source = right_values.at[:, pl.ds(j * BLOCK, BLOCK)]
+        right_loads.append(pltpu.make_async_copy(source, right_in.at[j], right_sem.at[j]))
+    for load in loads + right_loads:
+        load.start()
+    stage[:, slots] = jnp.zeros(stage.shape[:1] + stage.shape[2:], stage.dtype)
+
+    def chosen(ones, wanted):
+        found = [0] * wanted
+        count = 0
         for k, one in enumerate(ones):
-            block = candidate(k)
             for s in range(min(k + 1, wanted)):
-                if k == s:
-                    found[s] = block
-                else:
-                    found[s] = jnp.where((one != 0) & (before == s), block, found[s])
-            before = before + one
+                found[s] = jnp.where((one != 0) & (count == s), k, found[s])
+            count = count + one
         return found
 
     def unpick(one, before, packed):
@@ -161,24 +165,24 @@
             block = jnp.where((one != 0) & (before == s), value, block)
         return block
 
-    right_ones_load.wait()
-    ones = [right_pattern[col, row * col_blocks + j] for j in range(col_blocks)]
-    right_load.wait()
-    picks = pick(ones, slots, lambda j: right_in[:, j * BLOCK:(j + 1) * BLOCK])
-    for s in range(slots):
-        right_held[col, s] = picks[s]
-    pl.semaphore_wait(barrier, neighbours)
-    right.visit_own(start)
-
     left_ones_load.wait()
-    left_load.wait()
+    for load in loads:
+        load.wait()
     for b in range(left_blocks):
         ones = [left_pattern[row * group + k, col * left_blocks + b] for k in range(group)]
-        at = slice(b * BLOCK, (b + 1) * BLOCK)
-        picks = pick(ones, left_slots, lambda k: left_in[at, k * BLOCK:(k + 1) * BLOCK])
+        picks = chosen(ones, left_slots)
         for s in range(left_slots):
-            left_held[row, b, s] = picks[s]
+            left_held[row, b, s] = left_in[b, picks[s]]
+    pl.semaphore_wait(barrier, neighbours)
     left.visit_own(start)
+
+    right_ones_load.wait()
+    picks = chosen([right_pattern[col, row * col_blocks + j] for j in range(col_blocks)], slots)
+    for load in right_loads:
+        load.wait()
+    for s in range(slots):
+        right_held[col, s] = right_in[picks[s]]
+    right.visit_own(start)
 
     product[...] = jnp.zeros_like(product)
 
@@ -211,19 +215,19 @@
 
     def multiply(o):
         right.visit_inner(o, True, start)
-        ones, ranks = [], []
+        index = []
         for i in range(x_size):
             k = o * x_size + i
-            line = [right_pattern[k, row * col_blocks + j] for j in range(col_blocks)]
-            rank = [0] * col_blocks
-            for j in range(1, col_blocks):
-                rank[j] = rank[j - 1] + line[j - 1]
-            ones.append(line)
-            ranks.append(rank)
+            stage[i, :slots] = right_held[k]
+            count, line = 0, []
+            for j in range(col_blocks):
+                one = right_pattern[k, row * col_blocks + j]
+                line.append(jnp.where(one != 0, count, slots))
+                count = count + one
+            index.append(line)
 
         def dense(i, j):
-            packed = [right_held[o * x_size + i, s] for s in range(slots)]
-            return unpick(ones[i][j], ranks[i][j], packed)
+            return stage[i, index[i][j]]
 
         for j in range(0, col_blocks, 2):
             block = jnp.concatenate(
@@ -342,13 +346,16 @@
         scratch_shapes=[
             pltpu.SMEM(left_pattern.shape[::-1], jnp.int32),
             pltpu.SMEM(right_pattern.shape, jnp.int32),
-            pltpu.VMEM((rows_local, inner_local), jnp.bfloat16),
-            pltpu.VMEM((inner_rows, cols_local), jnp.bfloat16),
+            pltpu.VMEM((left_blocks, group, BLOCK, BLOCK), jnp.bfloat16),
+            pltpu.VMEM((col_blocks, BLOCK, BLOCK), jnp.bfloat16),
             pltpu.VMEM((row_count, left_blocks, left_slots, BLOCK, BLOCK), jnp.bfloat16),
             pltpu.VMEM((col_count, slots, BLOCK, BLOCK), jnp.bfloat16),
             pltpu.VMEM((inner // (x_size * BLOCK), rows_local, x_size * BLOCK), jnp.bfloat16),
+            pltpu.VMEM((x_size, slots + 1, BLOCK, BLOCK), jnp.bfloat16),
             pltpu.VMEM((col_count, col_blocks, BLOCK), jnp.float32),
-            dma((4,)),
+            dma((2,)),
+            dma((left_blocks, group)),
+            dma((col_blocks,)),
             dma((y_size, 1)),
             dma((2, row_count, 1)),
             dma((row_count, 1)),

time: 30.5 us -> 30.8 us (level)
  no operation moved by 1% of the time
where the time goes in v5:
time: 30.8 us; the launch traced here: 30.6 us
  Pallas kernels  28.9 us (94%)
  other arithmetic  1.71 us (6%)
    pallas_call x1, Pallas kernels, shards(): pl.pallas_call(functools.partial(kernel, (row_count, col_count, y_size, x...  28.9 us
    mul x1, other arithmetic, shards(): return product * product * scale  1.71 us

profile of v5, /device:TPU:0, one launch (start us, length us, event | category | flops | bytes accessed | tf_op | source)
XLA Modules:
  0.0 30.6 jit_solution(15341722829515645724)
XLA Ops:
  0.0 28.9 %shard_map.46 = (f32[512,1024]{1,0:T(8,128)S(1)}, f32[1,1024]{1,0:T(1,128)S(1)}) custom-call(s32[8,32]{1,0:T(8,128)} %bitcast.3, s32[8,32]{1,0:T(8,128)} %right_ones.1, bf16[512,256]{1,0:T(8,128)(2,1)} %left_values.1, bf16[128,1024]{1,0:T(8,128)(2,1)} %right_values.1), custom_call_target="tpu_custom_call" | custom-call | tf_op jit(solution)/shard_map/pallas_call | solution.py:338
  28.9 1.7 %multiply_multiply_fusion = f32[512,1024]{1,0:T(8,128)} fusion(f32[512,1024]{1,0:T(8,128)S(1)} %get-tuple-element.7, f32[1024]{0:T(1024)S(1)} %bitcast.2), kind=kLoop, calls=%fused_computation | loop fusion | flops 1048576 | bytes 4198400 | tf_op jit(solution)/shard_map/mul | solution.py:372

commit v6 on v3

--- a/solution.py
+++ b/solution.py
@@ -52,22 +52,19 @@
             for step in (1, -1):
                 self.each_inner(self.me, part, step, act)
 
-    def visit_outer(self, o, wait, act):
-        slot = o * self.inner + self.i
+    def visit_outer(self, distance, wait, act):
         for part in range(self.parts):
-            if wait:
-                self.copy(slot, part, 0, self.me).wait_recv()
-
-            @pl.when(o < self.o)
-            def _():
-                self.each_outer(slot, part, 1, act)
-
-            @pl.when(o > self.o)
-            def _():
-                self.each_outer(slot, part, -1, act)
-
-            for step in (1, -1):
-                self.each_inner(slot, part, step, act)
+            for sign in (-1, 1):
+                o = self.o + sign * distance
+
+                @pl.when((o >= 0) & (o < self.outer))
+                def _():
+                    slot = o * self.inner + self.i
+                    if wait:
+                        self.copy(slot, part, 0, self.me).wait_recv()
+                    self.each_outer(slot, part, -sign, act)
+                    for step in (1, -1):
+                        self.each_inner(slot, part, step, act)
 
     def visit_inner(self, o, wait, act):
         for distance in range(1, self.inner):
@@ -81,10 +78,6 @@
                         if wait:
                             self.copy(slot, part, 0, self.me).wait_recv()
                         self.each_inner(slot, part, -step, act)
-
-    def place(self, q):
-        o = jnp.where(q < self.outer, self.o - q, self.o + q - self.outer + 1)
-        return o, (o >= 0) & (o < self.outer)
 
     def greet(self, barrier):
         count = 0
@@ -137,10 +130,10 @@
     left_load = pltpu.make_async_copy(left_values, left_in, in_sem.at[1])
     left_ones_load = pltpu.make_async_copy(left_ones, left_pattern, in_sem.at[2])
     right_ones_load = pltpu.make_async_copy(right_ones, right_pattern, in_sem.at[3])
+    left_ones_load.start()
     right_ones_load.start()
+    left_load.start()
     right_load.start()
-    left_ones_load.start()
-    left_load.start()
 
     def pick(ones, wanted, candidate):
         before, found = 0, [None] * wanted
@@ -160,15 +153,6 @@
             block = jnp.where((one != 0) & (before == s), value, block)
         return block
 
-    right_ones_load.wait()
-    ones = [right_pattern[col, row * col_blocks + j] for j in range(col_blocks)]
-    right_load.wait()
-    picks = pick(ones, slots, lambda j: right_in[:, j * BLOCK:(j + 1) * BLOCK])
-    for s in range(slots):
-        right_held[col, s] = picks[s]
-    pl.semaphore_wait(barrier, neighbours)
-    right.visit_own(start)
-
     left_ones_load.wait()
     left_load.wait()
     for b in range(left_blocks):
@@ -177,18 +161,23 @@
         picks = pick(ones, left_slots, lambda k: left_in[at, k * BLOCK:(k + 1) * BLOCK])
         for s in range(left_slots):
             left_held[row, b, s] = picks[s]
+    pl.semaphore_wait(barrier, neighbours)
     left.visit_own(start)
 
+    right_ones_load.wait()
+    ones = [right_pattern[col, row * col_blocks + j] for j in range(col_blocks)]
+    right_load.wait()
+    picks = pick(ones, slots, lambda j: right_in[:, j * BLOCK:(j + 1) * BLOCK])
+    for s in range(slots):
+        right_held[col, s] = picks[s]
+    right.visit_own(start)
+
     product[...] = jnp.zeros_like(product)
 
     def finish_left():
-        @pl.loop(1, 2 * y_size - 1)
-        def _(q):
-            o, valid = left.place(q)
-
-            @pl.when(valid)
-            def _():
-                left.visit_outer(o, True, start)
+        @pl.loop(1, y_size)
+        def _(distance):
+            left.visit_outer(distance, True, start)
 
         @pl.loop(0, y_size)
         def _(o):
@@ -232,23 +221,26 @@
             at = pl.ds(j * BLOCK, 2 * BLOCK)
             product[:, at] += jnp.dot(left_dense[o], block, preferred_element_type=jnp.float32)
 
-    @pl.loop(0, 2 * z_size)
-    def _(q):
-        o, valid = right.place(q)
-
-        @pl.when((q > 0) & (q < 2 * z_size - 1) & valid)
+    lag = jnp.where((right.o > 0) & (right.o < z_size - 1), 2, 1)
+
+    @pl.loop(1, z_size + 2)
+    def _(t):
+        @pl.when(t < z_size)
         def _():
-            right.visit_outer(o, True, start)
-
-        @pl.when(q == 1)
+            right.visit_outer(t, True, start)
+
+        @pl.when(t == lag)
         def _():
             finish_left()
 
-        late, late_valid = right.place(jnp.maximum(q - 1, 0))
-
-        @pl.when((q >= 1) & late_valid)
-        def _():
-            multiply(late)
+        @pl.loop(0, 2)
+        def _(side):
+            distance = t - lag
+            o = right.o + (2 * side - 1) * distance
+
+            @pl.when((distance >= 0) & (distance + side > 0) & (o >= 0) & (o < z_size))
+            def _():
+                multiply(o)
 
     for j in range(col_blocks):
         part = product[:, j * BLOCK:(j + 1) * BLOCK]
@@ -271,25 +263,17 @@
     right.visit_own(wait_send)
     left.visit_own(wait_send)
 
-    @pl.loop(1, 2 * y_size - 1)
-    def _(q):
-        o, valid = left.place(q)
-
-        @pl.when(valid)
-        def _():
-            left.visit_outer(o, False, wait_send)
+    @pl.loop(1, y_size)
+    def _(distance):
+        left.visit_outer(distance, False, wait_send)
 
     @pl.loop(0, y_size)
     def _(o):
         left.visit_inner(o, False, wait_send)
 
-    @pl.loop(1, 2 * z_size - 1)
-    def _(q):
-        o, valid = right.place(q)
-
-        @pl.when(valid)
-        def _():
-            right.visit_outer(o, False, wait_send)
+    @pl.loop(1, z_size)
+    def _(distance):
+        right.visit_outer(distance, False, wait_send)
 
     @pl.loop(0, z_size)
     def _(o):

time: 34.5 us -> 27.1 us (0.79)
  Pallas kernels: 32.6 us -> 25.2 us
    pallas_call x1, Pallas kernels: 32.6 us -> 25.2 us  [shards(): pl.pallas_call(functools.partial(kernel, (row_count, col_count, y_size, x...]
where the time goes in v6:
time: 27.1 us; the launch traced here: 26.9 us
  Pallas kernels  25.2 us (93%)
  other arithmetic  1.71 us (6%)
    pallas_call x1, Pallas kernels, shards(): pl.pallas_call(functools.partial(kernel, (row_count, col_count, y_size, x...  25.2 us
    mul x1, other arithmetic, shards(): return product * product * scale  1.71 us

profile of v6, /device:TPU:0, one launch (start us, length us, event | category | flops | bytes accessed | tf_op | source)
XLA Modules:
  0.0 26.9 jit_solution(12780773183061808896)
XLA Ops:
  0.0 25.2 %shard_map.46 = (f32[512,1024]{1,0:T(8,128)S(1)}, f32[1,1024]{1,0:T(1,128)S(1)}) custom-call(s32[8,32]{1,0:T(8,128)} %bitcast.3, s32[8,32]{1,0:T(8,128)} %right_ones.1, bf16[512,256]{1,0:T(8,128)(2,1)} %left_values.1, bf16[128,1024]{1,0:T(8,128)(2,1)} %right_values.1), custom_call_target="tpu_custom_call" | custom-call | tf_op jit(solution)/shard_map/pallas_call | solution.py:317
  25.2 1.7 %multiply_multiply_fusion = f32[512,1024]{1,0:T(8,128)} fusion(f32[512,1024]{1,0:T(8,128)S(1)} %get-tuple-element.7, f32[1024]{0:T(1024)S(1)} %bitcast.2), kind=kLoop, calls=%fused_computation | loop fusion | flops 1048576 | bytes 4198400 | tf_op jit(solution)/shard_map/mul | solution.py:346

commit v7 on v6

--- a/solution.py
+++ b/solution.py
@@ -8,6 +8,7 @@
 from jax.sharding import PartitionSpec as P
 
 BLOCK = 128
+SCALE_STEPS = 8
 MESH = pl.DeviceIdType.MESH
 
 
@@ -300,6 +301,19 @@
         scale[0:1, j * BLOCK:(j + 1) * BLOCK] = factor[j:j + 1, :]
 
 
+def write_scaled(steps, product, scale, flow, scaled, sem):
+    depth = product.shape[0] // steps
+    writes = []
+    for step in range(steps):
+        at = pl.ds(step * depth, depth)
+        value = product[at, :]
+        scaled[at, :] = value * value * scale[...]
+        writes.append(pltpu.make_async_copy(scaled.at[at], flow.at[at], sem.at[step]))
+        writes[-1].start()
+    for write in writes:
+        write.wait()
+
+
 def shards(row_count, col_count, left_values, left_pattern, right_values, right_pattern):
     rows_local, inner_local = left_values.shape
     inner_rows, cols_local = right_values.shape
@@ -310,7 +324,7 @@
     left_blocks = rows_local // BLOCK
     col_blocks = cols_local // BLOCK
     slots = col_blocks // 2
-    parts = 2
+    parts = slots
     inner = row_count * inner_local
     dma = pltpu.SemaphoreType.DMA
     operands = (left_pattern.T, right_pattern, left_values, right_values)
@@ -343,7 +357,17 @@
             collective_id=0, has_side_effects=True, vmem_limit_bytes=32 * 1024 * 1024
         ),
     )(*(pltpu.with_memory_space_constraint(x, pltpu.HBM) for x in operands))
-    return product * product * scale
+    return pl.pallas_call(
+        functools.partial(write_scaled, SCALE_STEPS),
+        out_shape=jax.ShapeDtypeStruct((rows_local, cols_local), jnp.float32),
+        in_specs=[pl.BlockSpec(memory_space=pltpu.VMEM)] * 2,
+        out_specs=pl.BlockSpec(memory_space=pltpu.HBM),
+        scratch_shapes=[
+            pltpu.VMEM((rows_local, cols_local), jnp.float32),
+            dma((SCALE_STEPS,)),
+        ],
+        compiler_params=pltpu.CompilerParams(vmem_limit_bytes=8 * 1024 * 1024),
+    )(product, scale)
 
 
 def solution(mesh):

time: 27.1 us -> 27.3 us (level)
  Pallas kernels: 25.2 us -> 27.1 us
  other arithmetic: 1.71 us -> 0 us
    mul x1 -> x0, other arithmetic: 1.71 us -> none  [shards(): return product * product * scale]
    pallas_call x0 -> x1, Pallas kernels: none -> 1.4 us  [shards(): pl.pallas_call(functools.partial(write_scaled, SCALE_STEPS), out_shape=ja...]
    pallas_call x1, Pallas kernels: 25.2 us -> 25.7 us  [shards(): pl.pallas_call(functools.partial(kernel, (row_count, col_count, y_size, x...]
where the time goes in v7:
time: 27.3 us; the launch traced here: 27.1 us
  Pallas kernels  27.1 us (99%)
    pallas_call x1, Pallas kernels, shards(): pl.pallas_call(functools.partial(kernel, (row_count, col_count, y_size, x...  25.7 us
    pallas_call x1, Pallas kernels, shards(): pl.pallas_call(functools.partial(write_scaled, SCALE_STEPS), out_shape=ja...  1.4 us

profile of v7, /device:TPU:0, one launch (start us, length us, event | category | flops | bytes accessed | tf_op | source)
XLA Modules:
  0.0 27.1 jit_solution(17557735008893282684)
XLA Ops:
  0.0 25.7 %shard_map.46 = (f32[512,1024]{1,0:T(8,128)S(1)}, f32[1,1024]{1,0:T(1,128)S(1)}) custom-call(s32[8,32]{1,0:T(8,128)} %bitcast.1, s32[8,32]{1,0:T(8,128)} %right_ones.1, bf16[512,256]{1,0:T(8,128)(2,1)} %left_values.1, bf16[128,1024]{1,0:T(8,128)(2,1)} %right_values.1), custom_call_target="tpu_custom_call" | custom-call | tf_op jit(solution)/shard_map/pallas_call | solution.py:331
  25.7 1.4 %shard_map.47 = f32[512,1024]{1,0:T(8,128)} custom-call(f32[512,1024]{1,0:T(8,128)S(1)} %get-tuple-element.7.product, f32[1,1024]{1,0:T(1,128)S(1)} %get-tuple-element.8.scale), custom_call_target="tpu_custom_call" | custom-call | tf_op jit(solution)/shard_map/pallas_call | solution.py:360

commit v8 on v7

--- a/solution.py
+++ b/solution.py
@@ -162,8 +162,6 @@
         picks = pick(ones, left_slots, lambda k: left_in[at, k * BLOCK:(k + 1) * BLOCK])
         for s in range(left_slots):
             left_held[row, b, s] = picks[s]
-    pl.semaphore_wait(barrier, neighbours)
-    left.visit_own(start)
 
     right_ones_load.wait()
     ones = [right_pattern[col, row * col_blocks + j] for j in range(col_blocks)]
@@ -171,6 +169,8 @@
     picks = pick(ones, slots, lambda j: right_in[:, j * BLOCK:(j + 1) * BLOCK])
     for s in range(slots):
         right_held[col, s] = picks[s]
+    pl.semaphore_wait(barrier, neighbours)
+    left.visit_own(start)
     right.visit_own(start)
 
     product[...] = jnp.zeros_like(product)
@@ -222,6 +222,18 @@
             at = pl.ds(j * BLOCK, 2 * BLOCK)
             product[:, at] += jnp.dot(left_dense[o], block, preferred_element_type=jnp.float32)
 
+    def settle():
+        right.visit_own(wait_send)
+        left.visit_own(wait_send)
+
+        @pl.loop(1, y_size)
+        def _(distance):
+            left.visit_outer(distance, False, wait_send)
+
+        @pl.loop(0, y_size)
+        def _(o):
+            left.visit_inner(o, False, wait_send)
+
     lag = jnp.where((right.o > 0) & (right.o < z_size - 1), 2, 1)
 
     @pl.loop(1, z_size + 2)
@@ -233,6 +245,10 @@
         @pl.when(t == lag)
         def _():
             finish_left()
+
+        @pl.when(t == 2)
+        def _():
+            settle()
 
         @pl.loop(0, 2)
         def _(side):
@@ -260,17 +276,6 @@
     @pl.loop(1, col_count)
     def _(d):
         sum_copy(d).start()
-
-    right.visit_own(wait_send)
-    left.visit_own(wait_send)
-
-    @pl.loop(1, y_size)
-    def _(distance):
-        left.visit_outer(distance, False, wait_send)
-
-    @pl.loop(0, y_size)
-    def _(o):
-        left.visit_inner(o, False, wait_send)
 
     @pl.loop(1, z_size)
     def _(distance):
@@ -324,7 +329,7 @@
     left_blocks = rows_local // BLOCK
     col_blocks = cols_local // BLOCK
     slots = col_blocks // 2
-    parts = slots
+    parts = 2
     inner = row_count * inner_local
     dma = pltpu.SemaphoreType.DMA
     operands = (left_pattern.T, right_pattern, left_values, right_values)

time: 27.3 us -> 26.7 us (0.978)
  Pallas kernels: 27.1 us -> 26.5 us
    pallas_call x1, Pallas kernels: 25.7 us -> 25.1 us  [shards(): pl.pallas_call(functools.partial(kernel, (row_count, col_count, y_size, x...]
where the time goes in v8:
time: 26.7 us; the launch traced here: 26.5 us
  Pallas kernels  26.5 us (99%)
    pallas_call x1, Pallas kernels, shards(): pl.pallas_call(functools.partial(kernel, (row_count, col_count, y_size, x...  25.1 us
    pallas_call x1, Pallas kernels, shards(): pl.pallas_call(functools.partial(write_scaled, SCALE_STEPS), out_shape=ja...  1.4 us

profile of v8, /device:TPU:0, one launch (start us, length us, event | category | flops | bytes accessed | tf_op | source)
XLA Modules:
  0.0 26.5 jit_solution(17402997342578492899)
XLA Ops:
  0.0 25.1 %shard_map.46 = (f32[512,1024]{1,0:T(8,128)S(1)}, f32[1,1024]{1,0:T(1,128)S(1)}) custom-call(s32[8,32]{1,0:T(8,128)} %bitcast.1, s32[8,32]{1,0:T(8,128)} %right_ones.1, bf16[512,256]{1,0:T(8,128)(2,1)} %left_values.1, bf16[128,1024]{1,0:T(8,128)(2,1)} %right_values.1), custom_call_target="tpu_custom_call" | custom-call | tf_op jit(solution)/shard_map/pallas_call | solution.py:336
  25.1 1.4 %shard_map.47 = f32[512,1024]{1,0:T(8,128)} custom-call(f32[512,1024]{1,0:T(8,128)S(1)} %get-tuple-element.7.product, f32[1,1024]{1,0:T(1,128)S(1)} %get-tuple-element.8.scale), custom_call_target="tpu_custom_call" | custom-call | tf_op jit(solution)/shard_map/pallas_call | solution.py:365
